TPU v7x, 1024 devices: a whole 4x8x16 slice. The times are simulated.
1024 devices in a mesh: rows: 64 (over y, x, core), cols: 16 (over z).
Axes of the slice: x: 4, y: 8, z: 16, core: 2. Of those that a mesh axis runs over, the one named last changes fastest.
Arguments:
- fine_blocks: float32 [768, 7, 128, 128], P('rows'), may hold values from -0.5 to 0.5
- block_cols: int32 [768, 7], P('rows'), may hold values from 0 to 139, as said below
- row_length: int32 [768], P('rows'), may hold values from 4 to 7, as said below
- prolong: float32 [768, 2, 128, 128], P('rows', None, 'cols'), may hold values from -1.8 to 1.8
- aggregates: int32 [768, 2], P('rows'), may hold values from 0 to 191, as said below
- coarse_slot: int32 [768, 2, 7, 2], P('rows'), may hold values from 0 to 7
- send_plan: int32 [64, 64, 2], P('rows'), may hold values from -1 to 11, as said below
Outputs:
- coarse_blocks: float32 [192, 8, 128, 128], P('rows', None, 'cols')
Inputs may be any that keep to these rules, and one draw needn't show every extreme that they name: send_plan[q, p, c] is a fine row local to device q that q sends to device p in slot c, or -1 for an empty slot; the rows one device sends to another are distinct; no device sends to itself; each device receives 2 rows from exactly one other device, and 25 rows in all. block_cols of a live slot names a local row (below 12) or a received row 12 + q * 2 + c with send_plan[q, p, c] >= 0; every received row is named by some live slot; slot 0 names the row itself; slots at or beyond row_length name 0. `row_length`: slot 0 is always live; on every device, some row has 7 live slots and some has 4. aggregates[i, 0] is a coarse row of the device that holds fine row i (device p holds coarse rows p * 3 to p * 3 + 2), and each of those is named by some fine row of p; aggregates[i, 1] is a coarse row of another device, and the fine rows of one device name coarse rows of any one other device at most 1 times, exactly 1 times for some.
All inputs are finite; a program needn't handle non-finite values.
Results may differ from a plain program's by a relative error of at most 0.0001.
Values sent between devices are 32-bit elements; how exact they have to be, the bound alone decides.
A program may use at most 32 MiB of HBM per device.

v0:
```python
import jax
import jax.numpy as jnp
from jax import lax
from jax.sharding import PartitionSpec as P

KC = 8


PRECISE = lax.Precision.HIGHEST


def per_device(fine_blocks, block_cols, row_length, prolong, aggregates, coarse_slot, send_plan):
    peer_count = lax.axis_size("rows")
    fine_count = fine_blocks.shape[0]
    slot_count = fine_blocks.shape[1]
    coarse_count = fine_count // 4
    outbound_cap = (fine_count + peer_count - 2) // (peer_count - 1)
    sending = send_plan[0]
    present = (sending >= 0).astype(jnp.float32)
    packed = prolong[jnp.maximum(sending, 0)] * present[:, :, None, None, None]
    arrived = lax.all_to_all(packed, "rows", split_axis=0, concat_axis=0, tiled=True)
    row_pool = jnp.concatenate([prolong, arrived.reshape((-1,) + prolong.shape[1:])], axis=0)
    coupled = row_pool[block_cols]
    whole_prolong = lax.all_gather(prolong, "cols", axis=2, tiled=True)
    live_mask = (jnp.arange(slot_count)[None, :] < row_length[:, None]).astype(jnp.float32)
    slot_onehot = (coarse_slot[..., None] == jnp.arange(KC)[None, None, None, None, :]).astype(
        jnp.float32
    )
    slot_onehot = slot_onehot * live_mask[:, None, :, None, None]

    def triple(side):
        left_side = jnp.einsum(
            "ibr,ikrc->ikbc", whole_prolong[:, side], fine_blocks, precision=PRECISE
        )
        return jnp.einsum("iksac,ikbc->iksab", coupled, left_side, precision=PRECISE)

    def slotted(side):
        return jnp.einsum("ikse,iksab->ieab", slot_onehot[:, side], triple(side), precision=PRECISE)

    own_rows = slotted(0)
    own_onehot = (
        (aggregates[:, 0] % coarse_count)[:, None] == jnp.arange(coarse_count)[None, :]
    ).astype(jnp.float32)
    local_sum = jnp.einsum("ic,ieab->ceab", own_onehot, own_rows, precision=PRECISE)
    far_rows = slotted(1)
    target = aggregates[:, 1]
    dest_onehot = ((target // coarse_count)[:, None] == jnp.arange(peer_count)[None, :]).astype(
        jnp.int32
    )
    rank = jnp.sum(dest_onehot * (jnp.cumsum(dest_onehot, axis=0) - 1), axis=1)
    placing = dest_onehot[:, :, None] * (
        rank[:, None, None] == jnp.arange(outbound_cap)[None, None, :]
    ).astype(jnp.int32)
    outgoing = jnp.einsum(
        "inc,ieab->nceab", placing.astype(jnp.float32), far_rows, precision=PRECISE
    )
    out_tags = jnp.sum(placing * (target % coarse_count + 1)[:, None, None], axis=0) - 1
    incoming, in_tags = (
        lax.all_to_all(outgoing, "rows", split_axis=0, concat_axis=0, tiled=True),
        lax.all_to_all(out_tags, "rows", split_axis=0, concat_axis=0, tiled=True),
    )
    in_onehot = (in_tags[:, :, None] == jnp.arange(coarse_count)[None, None, :]).astype(jnp.float32)
    received = jnp.einsum("ncr,nceab->reab", in_onehot, incoming, precision=PRECISE)
    return local_sum + received


def solution(mesh):
    return jax.shard_map(
        per_device,
        mesh=mesh,
        in_specs=(
            P("rows", None, None, None),
            P("rows", None),
            P("rows"),
            P("rows", None, "cols", None),
            P("rows", None),
            P("rows", None, None, None),
            P("rows", None, None),
        ),
        out_specs=P("rows", None, "cols", None),
        check_vma=False,
    )
```

profile of v0, /device:TPU:1, one launch (start us, length us, event | category | flops | bytes accessed | tf_op | source)
XLA Modules:
  0.0 188.3 jit_solution(1297595144899277809)
XLA Ops:
  6.5 1.5 copy.52
  8.1 0.7 broadcast_maximum_fusion
  9.0 1.5 gather_fusion
  10.8 1.2 broadcast_multiply_fusion
  11.9 18.2 %all-to-all-start = ((f32[64,2,2,8,128]{4,3,2,1,0:T(8,128)}), f32[64,2,2,8,128]{4,3,2,1,0:T(8,128)S(1)}, u32[]{:S(2)}, u32[]{:S(2)}) async-start(f32[64,2,2,8,128]{4,3,2,1,0:T(8,128)} %broadcast_multiply_fusion), calls=%async_computation | async-start | bytes 2097152 | tf_op jit(solution)/shard_map/all_to_all | solution.py:21
  31.0 0.7 copy.56
  31.8 26.5 %all-to-all-done = f32[64,2,2,8,128]{4,3,2,1,0:T(8,128)S(1)} async-done(((f32[64,2,2,8,128]{4,3,2,1,0:T(8,128)}), f32[64,2,2,8,128]{4,3,2,1,0:T(8,128)S(1)}, u32[]{:S(2)}, u32[]{:S(2)}) %all-to-all-start) | async-done | bytes 1048608 | tf_op jit(solution)/shard_map/all_to_all | solution.py:21
  58.3 6.4 %all-to-all-start.1 = ((s32[64,1,1]{2,1,0:T(1,128)}), s32[64,1,1]{2,1,0:T(1,128)S(1)}, u32[]{:S(2)}, u32[]{:S(2)}) async-start(s32[64,1,1]{2,1,0:T(1,128)} %copy.56), calls=%async_computation.1 | async-start | bytes 65536 | tf_op jit(solution)/shard_map/all_to_all | solution.py:60
  64.8 0.7 gather_fusion.1
  65.5 22.9 %all-gather.2.cloned.1.call-done = f32[12,2,128,128]{3,2,0,1:T(8,128)} async-done(((f32[12,2,8,128]{3,2,0,1:T(8,128)}), f32[12,2,128,128]{3,2,0,1:T(8,128)}) %all-gather.2.cloned.1.call-update) | async-done | bytes 1572880 | tf_op jit(solution)/shard_map/all_gather | solution.py:24
  88.5 11.1 %fusion.10 = f32[12,7,128,128]{3,2,1,0:T(8,128)S(1)} fusion(f32[12,7,128,128]{3,2,1,0:T(8,128)} %param.7, f32[12,2,128,128]{3,2,0,1:T(8,128)} %all-gather.2.cloned.1.call-done), kind=kOutput, calls=%fused_computation.15 | convolution fusion | flops 2113929216 | bytes 11796480 | tf_op jit(solution)/shard_map/ibr,ikrc->ikbc/dot_general | solution.py:32
  99.6 4.9 %fusion = f32[12,7,2,8,128]{4,3,2,1,0:T(8,128)S(1)} fusion(f32[12,7,2,8,128]{4,3,2,1,0:T(8,128)S(1)} %bitcast.81, f32[12,7,128,128]{3,2,1,0:T(8,128)S(1)} %fusion.10), kind=kOutput, calls=%fused_computation.2 | convolution fusion | flops 264241152 | bytes 6881280 | tf_op jit(solution)/shard_map/iksac,ikbc->iksab/dot_general | solution.py:35
  104.4 0.8 convolution_bitcast_fusion.1
  105.2 1.9 %convolution_bitcast_fusion = f32[64,1,8,8,128]{4,0,3,2,1:T(8,128)S(1)} fusion(f32[12,8,8,128]{3,1,2,0:T(8,128)S(1)} %convolution_bitcast_fusion.1, s32[12]{0:T(128)S(1)} %compare_convert_fusion, s32[12]{0:T(128)S(1)} %get-tuple-element.5), kind=kOutput, calls=%fused_computation.9 | convolution fusion | flops 75499776 | bytes 2490464 | tf_op jit(solution)/shard_map/inc,ieab->nceab/dot_general | solution.py:54
  107.1 2.5 %copy.60 = f32[64,1,8,8,128]{4,3,2,1,0:T(8,128)} copy(f32[64,1,8,8,128]{4,0,3,2,1:T(8,128)S(1)} %convolution_bitcast_fusion) | data formatting | bytes 4194304 | tf_op jit(solution)/shard_map/inc,ieab->nceab/dot_general | solution.py:54
  109.7 19.5 %all-to-all-start.2 = ((f32[64,1,8,8,128]{4,3,2,1,0:T(8,128)}), f32[64,1,8,8,128]{4,3,2,1,0:T(8,128)S(1)}, u32[]{:S(2)}, u32[]{:S(2)}) async-start(f32[64,1,8,8,128]{4,3,2,1,0:T(8,128)} %copy.60), calls=%async_computation.2 | async-start | bytes 4194304 | tf_op jit(solution)/shard_map/all_to_all | solution.py:59
  129.2 1.2 reduce.1
  130.4 11.2 %fusion.11 = f32[12,7,128,128]{3,2,1,0:T(8,128)S(1)} fusion(f32[12,7,128,128]{3,2,1,0:T(8,128)} %param.7, f32[12,2,128,128]{3,2,0,1:T(8,128)} %all-gather.2.cloned.1.call-done), kind=kOutput, calls=%fused_computation.17 | convolution fusion | flops 2113929216 | bytes 11796480 | tf_op jit(solution)/shard_map/ibr,ikrc->ikbc/dot_general | solution.py:32
  141.6 4.9 %fusion.2 = f32[12,7,2,8,128]{4,3,2,1,0:T(8,128)S(1)} fusion(f32[12,7,2,8,128]{4,3,2,1,0:T(8,128)S(1)} %bitcast.82, f32[12,7,128,128]{3,2,1,0:T(8,128)S(1)} %fusion.11), kind=kOutput, calls=%fused_computation.4 | convolution fusion | flops 264241152 | bytes 6881280 | tf_op jit(solution)/shard_map/iksac,ikbc->iksab/dot_general | solution.py:35
  146.5 0.8 convolution_bitcast_fusion.2
  147.2 0.5 fusion.15
  147.7 31.1 %all-to-all-done.2 = f32[64,1,8,8,128]{4,3,2,1,0:T(8,128)S(1)} async-done(((f32[64,1,8,8,128]{4,3,2,1,0:T(8,128)}), f32[64,1,8,8,128]{4,3,2,1,0:T(8,128)S(1)}, u32[]{:S(2)}, u32[]{:S(2)}) %all-to-all-start.2) | async-done | bytes 2097184 | tf_op jit(solution)/shard_map/all_to_all | solution.py:59
  178.8 2.0 %fusion.7 = f32[3,8,8,128]{3,0,2,1:T(4,128)S(1)} fusion(f32[3,8,8,128]{3,0,2,1:T(4,128)S(1)} %fusion.15, f32[64,1,8,8,128]{4,3,2,1,0:T(8,128)S(1)} %all-to-all-done.2, s32[64]{0:T(128)S(1)} %reduce.1), kind=kOutput, calls=%fused_computation.13 | convolution fusion | flops 18899136 | bytes 2294016 | tf_op jit(solution)/shard_map/ncr,nceab->reab/dot_general | solution.py:63
  180.8 0.6 copy.62
  (36 shorter events, 1.3 us)
Async XLA Ops:
  6.5 4.1 %copy-start.3 = (s32[1,64,2]{1,2,0:T(2,128)S(1)}, s32[1,64,2]{1,2,0:T(2,128)}, u32[]{:S(2)}) copy-start(s32[1,64,2]{1,2,0:T(2,128)} %param.13) | copy-start | bytes 1540
  6.5 81.9 %all-gather.2.cloned.1.call-start = ((), (), s32[]{:S(2)}) async-start(), calls=%async_computation.3 | async-start | bytes 1671168 | tf_op jit(solution)/shard_map/all_gather | solution.py:24
  10.7 19.5 %copy-start.2 = (s32[12,7]{0,1:T(8,128)S(1)}, s32[12,7]{0,1:T(8,128)}, u32[]{:S(2)}) copy-start(s32[12,7]{0,1:T(8,128)} %param.8) | copy-start | bytes 1012
  10.7 19.7 %copy-start.1 = (s32[12,2,7,2]{0,3,2,1:T(2,128)S(1)}, s32[12,2,7,2]{0,3,2,1:T(2,128)}, u32[]{:S(2)}) copy-start(s32[12,2,7,2]{0,3,2,1:T(2,128)} %param.12) | copy-start | bytes 4036
  10.7 19.8 %copy-start.4 = (s32[12,2]{0,1:T(2,128)S(1)}, s32[12,2]{0,1:T(2,128)}, u32[]{:S(2)}) copy-start(s32[12,2]{0,1:T(2,128)} %param.11) | copy-start | bytes 292
  10.7 20.9 %copy-start.5 = (s32[12]{0:T(128)S(1)}, s32[12]{0:T(128)}, u32[]{:S(2)}) copy-start(s32[12]{0:T(128)} %param.9) | copy-start | bytes 148
  10.7 54.0 %copy-start = (f32[12,2,8,128]{3,2,1,0:T(8,128)S(1)}, f32[12,2,8,128]{3,2,1,0:T(8,128)}, u32[]{:S(2)}) copy-start(f32[12,2,8,128]{3,2,1,0:T(8,128)} %param.10) | copy-start | bytes 294916
  11.9 46.4 %all-to-all-start = ((f32[64,2,2,8,128]{4,3,2,1,0:T(8,128)}), f32[64,2,2,8,128]{4,3,2,1,0:T(8,128)S(1)}, u32[]{:S(2)}, u32[]{:S(2)}) async-start(f32[64,2,2,8,128]{4,3,2,1,0:T(8,128)} %broadcast_multiply_fusion), calls=%async_computation | async-start | bytes 2097152 | tf_op jit(solution)/shard_map/all_to_all | solution.py:21
  58.3 51.3 %all-to-all-start.1 = ((s32[64,1,1]{2,1,0:T(1,128)}), s32[64,1,1]{2,1,0:T(1,128)S(1)}, u32[]{:S(2)}, u32[]{:S(2)}) async-start(s32[64,1,1]{2,1,0:T(1,128)} %copy.56), calls=%async_computation.1 | async-start | bytes 65536 | tf_op jit(solution)/shard_map/all_to_all | solution.py:60
  109.7 69.2 %all-to-all-start.2 = ((f32[64,1,8,8,128]{4,3,2,1,0:T(8,128)}), f32[64,1,8,8,128]{4,3,2,1,0:T(8,128)S(1)}, u32[]{:S(2)}, u32[]{:S(2)}) async-start(f32[64,1,8,8,128]{4,3,2,1,0:T(8,128)} %copy.60), calls=%async_computation.2 | async-start | bytes 4194304 | tf_op jit(solution)/shard_map/all_to_all | solution.py:59
Sparse Core Ops, SparseCore 0:
  9.9 78.4 all-gather.1
where the time goes:
time: 189 us; the launch traced here: 188 us
  waiting for transfers between devices  80.6 us (43%)
  starting transfers between devices  44.1 us (23%)
  matrix products  37.9 us (20%)
  between operations  13.6 us (7%)
  local copies, waits for them, and re-layouts  8.31 us (4%)
  other arithmetic  3.71 us (2%)
    all_to_all x1, waiting for transfers between devices, per_device(): lax.all_to_all(outgoing, 'rows', split_axis=0, concat_axis=0, tiled=True)  31.1 us
    all_to_all x1, waiting for transfers between devices, per_device(): lax.all_to_all(packed, 'rows', split_axis=0, concat_axis=0, tiled=True)  26.5 us
    all_gather x1, waiting for transfers between devices, per_device(): whole_prolong = lax.all_gather(prolong, 'cols', axis=2, tiled=True)  22.9 us
    dot_general x2, matrix products, triple(): jnp.einsum('ibr,ikrc->ikbc', whole_prolong[:, side], fine_blocks, precisi...  22.3 us
    all_to_all x1, starting transfers between devices, per_device(): lax.all_to_all(outgoing, 'rows', split_axis=0, concat_axis=0, tiled=True)  19.5 us
    all_to_all x1, starting transfers between devices, per_device(): lax.all_to_all(packed, 'rows', split_axis=0, concat_axis=0, tiled=True)  18.2 us
    dot_general x2, matrix products, triple(): jnp.einsum('iksac,ikbc->iksab', coupled, left_side, precision=PRECISE)  9.73 us
    all_to_all x1, starting transfers between devices, per_device(): lax.all_to_all(out_tags, 'rows', split_axis=0, concat_axis=0, tiled=True)  6.42 us
  transfers between devices with their start and end apart: 4, of which 3 were waited for; matrix products, arithmetic and copies ran while one was open for 24% of the time, Pallas kernels for 0%

commit v1 on v0

v1 whole, which is shorter than its diff:
```python
import functools

import jax
import jax.numpy as jnp
from jax import lax
from jax.experimental import pallas as pl
from jax.experimental.pallas import tpu as pltpu
from jax.sharding import PartitionSpec as P

NX, NC = 4, 2
KC = 8
CR = 3
A8 = 8
LANES = 128
HALVES = 2
PARTS = 2
F32, BF16 = jnp.float32, jnp.bfloat16
NT = (((1,), (1,)), ((), ()))
NN = (((1,), (0,)), ((), ()))
MESH = pl.DeviceIdType.MESH


def split(v):
    high = v.astype(BF16)
    return high, (v - high.astype(F32)).astype(BF16)


def wide(v):
    high, low = split(v)
    return jnp.concatenate(
        [jnp.concatenate([high, high], axis=1), jnp.concatenate([low, jnp.zeros_like(low)], axis=1)], axis=0
    )


def steps_of(count, half):
    plus = count // 2 if half % 2 == 0 else count // 2 - 1
    return plus, count - 1 - plus


def ring_ids(count, halves):
    ids = {}
    for half in range(halves):
        for way, steps in zip((1, -1), steps_of(count, half)):
            for step in range(steps):
                ids[half, way, step] = len(ids)
    return ids


def kernel(
    dims, fine, prolong, tab, slots, pool_at, own_tag, out,
    blocks, cut, whole, column, tabs, tabs_s, picked, pool, applied, far, own, acc, crossed, running,
    local_sem, tab_send, tab_recv, z_send, z_recv, y_send, y_recv, g_send, g_recv,
    x_send, x_recv, c_send, c_recv, r_send, r_recv,
):
    NY, NZ, FR, KA = dims
    group = NX * NC
    per = NY + 1
    NB = NZ * A8
    EC = KC // HALVES
    hr = FR // HALVES
    pr = FR // PARTS
    row, z = lax.axis_index("rows"), lax.axis_index("cols")
    core, x, y = row % NC, (row // NC) % NX, row // group
    here = x * NC + core

    def rid(yy, xx, cc):
        return (yy * NX + xx) * NC + cc

    def copy(src, dst, send, recv, device):
        return pltpu.make_async_remote_copy(
            src_ref=src, dst_ref=dst, send_sem=send, recv_sem=recv, device_id=device, device_id_type=MESH
        )

    def z_dev(way):
        return (row, (z + way + NZ) % NZ)

    def y_dev(way):
        return (rid((y + way + NY) % NY, x, core), z)

    def x_dev(way):
        return (rid(y, (x + way + NX) % NX, core), z)

    def g_dev(o):
        return (rid(y, (x + o // NC) % NX, (core + o % NC) % NC), z)

    core_dev = (rid(y, x, (core + 1) % NC), z)

    load = pltpu.make_async_copy(fine, blocks, local_sem.at[0])
    load.start()

    barrier = pltpu.get_barrier_semaphore()
    partners = [z_dev(o) for o in sorted({1, NZ - 1})]
    partners += [y_dev(o) for o in range(1, NY)]
    partners += [g_dev(o) for o in range(1, group)]
    for device in partners:
        pl.semaphore_signal(barrier, inc=1, device_id=device, device_id_type=MESH)
    pl.semaphore_wait(barrier, len(partners))

    sent = []

    def go(c):
        c.start()
        sent.append(c)

    z_ids, y_ids, x_ids = ring_ids(NZ, HALVES), ring_ids(NY, HALVES), ring_ids(NX, HALVES)

    def rows_of(half):
        return pl.ds(half * hr, hr)

    def ring_send(buf, ids, send, recv, me, count, dev, half, way, step):
        at = (me - way * step + count) % count
        part = prolong.at[rows_of(half)] if step == 0 else buf.at[at, rows_of(half)]
        n = ids[half, way, step]
        go(copy(part, buf.at[at, rows_of(half)], send.at[n], recv.at[n], dev(way)))

    def ring_wait(buf, ids, send, recv, me, count, dev, half, way, step):
        at = (me - way * (step + 1) + 2 * count) % count
        part = buf.at[at, rows_of(half)]
        n = ids[half, way, step]
        copy(part, part, send.at[n], recv.at[n], dev(way)).wait_recv()

    zr = (whole, z_ids, z_send, z_recv, z, NZ, z_dev)
    yr = (column, y_ids, y_send, y_recv, y, NY, y_dev)

    def advance(ring, ids, step):
        for half in range(HALVES):
            for way in (1, -1):
                if (half, way, step) in ids:
                    ring_wait(*ring, half, way, step)
                    if (half, way, step + 1) in ids:
                        ring_send(*ring, half, way, step + 1)

    for half in range(HALVES):
        for way in (1, -1):
            if (half, way, 0) in y_ids:
                ring_send(*yr, half, way, 0)
    for o in range(1, NY):
        go(copy(tab, tabs.at[y], tab_send.at[o], tab_recv.at[o], y_dev(o)))
    for o in range(1, NX):
        go(copy(tab, tabs.at[NY + x], tab_send.at[NY + o], tab_recv.at[NY + o], x_dev(o)))
    for half in range(HALVES):
        for way in (1, -1):
            if (half, way, 0) in z_ids:
                ring_send(*zr, half, way, 0)

    mine = prolong[...]
    whole[z] = mine
    column[y] = mine
    pool[pl.ds(0, FR)] = mine
    tabs[y] = tab[...]
    tabs[NY + x] = tab[...]

    load.wait()

    @pl.loop(0, FR)
    def _(i):
        for k in range(KA):
            high, low = split(blocks[i * KA + k])
            cut[i * KA + k] = jnp.concatenate([high, low], axis=1)

    advance(yr, y_ids, 0)
    advance(zr, z_ids, 0)
    for o in range(1, NY):
        at = tabs.at[(y - o + NY) % NY]
        copy(at, at, tab_send.at[o], tab_recv.at[o], y_dev(o)).wait_recv()
    for o in range(1, NX):
        at = tabs.at[NY + (x - o + NX) % NX]
        copy(at, at, tab_send.at[NY + o], tab_recv.at[NY + o], x_dev(o)).wait_recv()
    to_scalar = pltpu.make_async_copy(tabs, tabs_s, local_sem.at[1])
    to_scalar.start()
    y_steps = NY // 2
    for step in range(1, y_steps):
        advance(yr, y_ids, step)
        advance(zr, z_ids, step)
    to_scalar.wait()

    def pick(o, put):
        dest = rid(y, (x + o // NC) % NX, (core + o % NC) % NC)
        second_y, second_row = 0, 0
        for yy in range(NY):
            put(yy, column[yy, tabs_s[yy, 0, dest]])
            extra = tabs_s[yy, 1, dest]
            second_y = jnp.where(extra > 0, yy, second_y)
            second_row = jnp.where(extra > 0, extra - 1, second_row)
        put(NY, column[second_y, second_row])

    for o in list(range(1, group)) + [0]:
        if o:
            def put(n, v, o=o):
                picked[o, n] = v
        else:
            def put(n, v):
                pool[FR + here * per + n] = v
        pick(o, put)
        if o:
            go(copy(
                picked.at[o], pool.at[pl.ds(FR + here * per, per)], g_send.at[o], g_recv.at[o], g_dev(o)
            ))

    z_steps = NZ // 2
    for step in range(y_steps, z_steps - 1):
        advance(zr, z_ids, step)
    for o in range(1, group):
        src = ((x - o // NC + NX) % NX) * NC + (core - o % NC + NC) % NC
        at = pool.at[pl.ds(FR + src * per, per)]
        copy(at, at, g_send.at[o], g_recv.at[o], g_dev(o)).wait_recv()
    if z_steps > y_steps:
        advance(zr, z_ids, z_steps - 1)

    r8 = lax.broadcasted_iota(jnp.int32, (KC * A8, LANES), 0)
    l8 = lax.broadcasted_iota(jnp.int32, (KC * A8, LANES), 1)
    same_a, slot_of = (r8 % A8) == (l8 % A8), r8 // A8

    def couple(i):
        for k in range(KA):
            lhs = wide(pool[pool_at[i * KA + k]].reshape(2 * A8, LANES))
            both = lax.dot_general(lhs, cut[i * KA + k], NT, preferred_element_type=F32)
            applied[i, 2 * A8 * k:2 * A8 * (k + 1)] = both[:2 * A8] + both[2 * A8:]
        applied[i, 2 * A8 * KA:] = jnp.zeros((LANES - 2 * A8 * KA, LANES), F32)

    def product(i, t):
        xh, xl = split(applied[i])
        where = jnp.where(same_a & (slots[i * 2 + t][None, :] == slot_of), 1.0, 0.0).astype(BF16)
        summed = lax.dot_general(
            jnp.concatenate([where, where], axis=1), jnp.concatenate([xh, xl], axis=0), NN,
            preferred_element_type=F32,
        )
        high, low = split(whole[:, i, t].reshape(NB, LANES))
        both = lax.dot_general(
            wide(summed), jnp.concatenate([high, low], axis=1), NT, preferred_element_type=F32
        )
        return (both[:KC * A8] + both[KC * A8:]).reshape(KC, A8, NB)

    def x_send_go(p, half, way, step):
        at = far.at[half, (x - way * step + NX) % NX, pl.ds(p * pr, pr)]
        n = p * len(x_ids) + x_ids[half, way, step]
        go(copy(at, at, x_send.at[n], x_recv.at[n], x_dev(way)))

    def x_wait(p, half, way, step):
        at = far.at[half, (x - way * (step + 1) + 2 * NX) % NX, pl.ds(p * pr, pr)]
        n = p * len(x_ids) + x_ids[half, way, step]
        copy(at, at, x_send.at[n], x_recv.at[n], x_dev(way)).wait_recv()

    def x_advance(p, step):
        for half in range(HALVES):
            for way in (1, -1):
                if (half, way, step) in x_ids:
                    x_wait(p, half, way, step)
                    if (half, way, step + 1) in x_ids:
                        x_send_go(p, half, way, step + 1)

    for p in range(PARTS):
        @pl.loop(p * pr, (p + 1) * pr)
        def _(i):
            couple(i)
            made = product(i, 1)
            for half in range(HALVES):
                far[half, x, i] = made[half * EC:(half + 1) * EC]

        for half in range(HALVES):
            for way in (1, -1):
                if (half, way, 0) in x_ids:
                    x_send_go(p, half, way, 0)

    own[...] = jnp.zeros_like(own)
    for p in range(PARTS):
        @pl.loop(p * pr, (p + 1) * pr)
        def _(i):
            made = product(i, 0)
            for c in range(CR):
                own[c] += made * jnp.where(own_tag[i] == c, 1.0, 0.0)

        x_advance(p, 0)
    for step in range(1, NX // 2):
        for p in range(PARTS):
            x_advance(p, step)

    for half in range(HALVES):
        for cc in range(NC):
            @pl.loop(0, NY)
            def _(yy):
                dest = rid(yy, x, cc)
                sums = [jnp.zeros((EC, A8, NB), F32) for _ in range(CR)]
                for xx in range(NX):
                    rows = far[half, xx, tabs_s[NY + xx, 2, dest]]
                    tag = tabs_s[NY + xx, 3, dest]
                    for c in range(CR):
                        sums[c] += rows * jnp.where(tag == c + 1, 1.0, 0.0)
                for c in range(CR):
                    acc[cc, half, yy, c] = sums[c]

        go(copy(acc.at[(core + 1) % NC, half], crossed.at[half], c_send.at[half], c_recv.at[half], core_dev))

    r_ids = ring_ids(NY, HALVES)

    def run(half, way, step):
        far_end = steps_of(NY, half)[0 if way == 1 else 1]
        dest = (y + way * (far_end - step) + 2 * NY) % NY
        n = r_ids[half, way, step]
        total = crossed[half, dest] + acc[core, half, dest]
        if step:
            total += running[r_ids[half, way, step - 1]]
        crossed[half, dest] = total
        go(copy(crossed.at[half, dest], running.at[n], r_send.at[n], r_recv.at[n], y_dev(way)))

    def run_wait(half, way, step):
        n = r_ids[half, way, step]
        copy(running.at[n], running.at[n], r_send.at[n], r_recv.at[n], y_dev(way)).wait_recv()

    for half in range(HALVES):
        at = crossed.at[half]
        copy(at, at, c_send.at[half], c_recv.at[half], core_dev).wait_recv()
        for way in (1, -1):
            if (half, way, 0) in r_ids:
                run(half, way, 0)
    for step in range(y_steps):
        for half in range(HALVES):
            for way in (1, -1):
                if (half, way, step) in r_ids:
                    run_wait(half, way, step)
                    if (half, way, step + 1) in r_ids:
                        run(half, way, step + 1)
    for half in range(HALVES):
        total = own[:, half * EC:(half + 1) * EC] + crossed[half, y] + acc[core, half, y]
        for way, steps in zip((1, -1), steps_of(NY, half)):
            if steps:
                total += running[r_ids[half, way, steps - 1]]
        out[:, half * EC:(half + 1) * EC] = total

    for c in sent:
        c.wait_send()


def per_device(fine_blocks, block_cols, row_length, prolong, aggregates, coarse_slot, send_plan):
    peers, NZ = lax.axis_size("rows"), lax.axis_size("cols")
    FR, KA = fine_blocks.shape[:2]
    group = NX * NC
    NY = peers // group
    per = NY + 1
    NB = NZ * A8
    EC = KC // HALVES

    plan = send_plan[0]
    first, second = plan[:, 0], plan[:, 1]
    main = jnp.where(first >= 0, first, jnp.maximum(second, 0))
    extra = jnp.where((first >= 0) & (second >= 0), second + 1, 0)
    target = aggregates[:, 1]
    hit = ((target // CR)[:, None] == jnp.arange(peers)[None, :]).astype(jnp.int32)
    held = jnp.sum(hit * jnp.arange(FR)[:, None], axis=0)
    tag = jnp.sum(hit * (target % CR + 1)[:, None], axis=0)
    tab = jnp.pad(jnp.stack([main, extra, held, tag]), ((0, 4), (0, LANES - peers))).astype(jnp.int32)

    live = jnp.arange(KA)[None, :] < row_length[:, None]
    cols, alive = block_cols.reshape(-1), live.reshape(-1)
    ghost = jnp.maximum(cols - FR, 0)
    source, at = ghost // 2, ghost % 2
    paired = jnp.any((cols[None, :] == cols[:, None] - 1) & alive[None, :], axis=1) & (at == 1)
    place = jnp.where(paired, NY, source // group)
    pool_at = jnp.where(cols < FR, cols, FR + (source % group) * per + place).astype(jnp.int32)

    slots = jnp.where(live[:, None, :, None], coarse_slot, -1).reshape(FR * 2, KA * 2)
    slots = jnp.repeat(slots, A8, axis=1)
    slots = jnp.pad(slots, ((0, 0), (0, LANES - slots.shape[1])), constant_values=-1)

    vm, sm = pl.BlockSpec(memory_space=pltpu.VMEM), pl.BlockSpec(memory_space=pltpu.SMEM)
    count_z, count_y = len(ring_ids(NZ, HALVES)), len(ring_ids(NY, HALVES))
    count_x = len(ring_ids(NX, HALVES)) * PARTS
    dma = pltpu.SemaphoreType.DMA
    return pl.pallas_call(
        functools.partial(kernel, (NY, NZ, FR, KA)),
        out_shape=jax.ShapeDtypeStruct((CR, KC, A8, NB), F32),
        in_specs=[pl.BlockSpec(memory_space=pl.ANY), vm, vm, vm, sm, sm],
        out_specs=vm,
        scratch_shapes=[
            pltpu.VMEM((FR * KA, LANES, LANES), F32),
            pltpu.VMEM((FR * KA, LANES, 2 * LANES), BF16),
            pltpu.VMEM((NZ, FR, 2, A8, LANES), F32),
            pltpu.VMEM((NY, FR, 2, A8, LANES), F32),
            pltpu.VMEM((NY + NX, 8, LANES), jnp.int32),
            pltpu.SMEM((NY + NX, 8, LANES), jnp.int32),
            pltpu.VMEM((group, per, 2, A8, LANES), F32),
            pltpu.VMEM((FR + group * per, 2, A8, LANES), F32),
            pltpu.VMEM((FR, LANES, LANES), F32),
            pltpu.VMEM((HALVES, NX, FR, EC, A8, NB), F32),
            pltpu.VMEM((CR, KC, A8, NB), F32),
            pltpu.VMEM((NC, HALVES, NY, CR, EC, A8, NB), F32),
            pltpu.VMEM((HALVES, NY, CR, EC, A8, NB), F32),
            pltpu.VMEM((count_y, CR, EC, A8, NB), F32),
            dma((2,)), dma((NY + NX,)), dma((NY + NX,)), dma((count_z,)), dma((count_z,)),
            dma((count_y,)), dma((count_y,)), dma((group,)), dma((group,)),
            dma((count_x,)), dma((count_x,)), dma((HALVES,)), dma((HALVES,)),
            dma((count_y,)), dma((count_y,)),
        ],
        compiler_params=pltpu.CompilerParams(
            collective_id=0, has_side_effects=True, vmem_limit_bytes=48 * 2**20
        ),
    )(
        fine_blocks.reshape(FR * KA, LANES, LANES), prolong, tab, slots, pool_at,
        (aggregates[:, 0] % CR).astype(jnp.int32),
    )


def solution(mesh):
    return jax.shard_map(
        per_device,
        mesh=mesh,
        in_specs=(
            P("rows", None, None, None),
            P("rows", None),
            P("rows"),
            P("rows", None, "cols", None),
            P("rows", None),
            P("rows", None, None, None),
            P("rows", None, None),
        ),
        out_specs=P("rows", None, "cols", None),
        check_vma=False,
    )
```

time: 189 us -> 95.7 us (0.51)
  Pallas kernels: 0 us -> 85.3 us
  waiting for transfers between devices: 80.6 us -> 0 us
  starting transfers between devices: 44.1 us -> 0 us
  matrix products: 37.9 us -> 0 us
  between operations: 13.6 us -> 0.06 us
  local copies, waits for them, and re-layouts: 8.31 us -> 5.52 us
    pallas_call x0 -> x1, Pallas kernels: none -> 85.3 us  [per_device(): pl.pallas_call(functools.partial(kernel, (NY, NZ, FR, KA)), out_shape=jax...]
    all_to_all x3 -> x0, waiting for transfers between devices: 57.6 us -> none  [the longest x1 31.1 us: per_device(): lax.all_to_all(outgoing, 'rows', split_axis=0, concat_axis=0, tiled=True)]
    all_to_all x3 -> x0, starting transfers between devices: 44.1 us -> none  [the longest x1 19.5 us: per_device(): lax.all_to_all(outgoing, 'rows', split_axis=0, concat_axis=0, tiled=True)]
    dot_general x9 -> x0, matrix products: 37.9 us -> none  [the longest x2 22.3 us: triple(): jnp.einsum('ibr,ikrc->ikbc', whole_prolong[:, side], fine_blocks, precisi...]
    all_gather x1 -> x0, waiting for transfers between devices: 22.9 us -> none  [per_device(): whole_prolong = lax.all_gather(prolong, 'cols', axis=2, tiled=True)]
    unnamed x14 -> x6, local copies, waits for them, and re-layouts: 1.69 us -> 4.89 us
    dot_general x1 -> x0, local copies, waits for them, and re-layouts: 2.54 us -> none  [per_device(): jnp.einsum('inc,ieab->nceab', placing.astype(jnp.float32), far_rows, prec...]
    gather x2 -> x0, local copies, waits for them, and re-layouts: 2.21 us -> none  [the longest x1 1.54 us: per_device(): packed = prolong[jnp.maximum(sending, 0)] * present[:, :, None, None, None]]
  transfers between devices with their start and end apart: 4 -> 0, of which waited for: 3 -> 0; matrix products, arithmetic and copies ran while one was open for 24% -> 0% of each run, Pallas kernels for 0% -> 0%
where the time goes in v1:
time: 95.7 us; the launch traced here: 94.8 us
  Pallas kernels  85.3 us (89%)
  local copies, waits for them, and re-layouts  5.52 us (6%)
  other arithmetic  3.91 us (4%)
    pallas_call x1, Pallas kernels, per_device(): pl.pallas_call(functools.partial(kernel, (NY, NZ, FR, KA)), out_shape=jax...  85.3 us
    unnamed x6, local copies, waits for them, and re-layouts  4.89 us

profile of v1, /device:TPU:1, one launch (start us, length us, event | category | flops | bytes accessed | tf_op | source)
XLA Modules:
  0.0 94.8 jit_solution(9705994095970042636)
XLA Ops:
  0.0 0.7 and_select_fusion.own_tag
  0.7 0.8 compare_select_fusion.1
  1.4 0.7 fusion.2
  2.1 0.1 select_reduce_fusion.1
  2.2 0.7 iota_compare_fusion
  3.0 0.1 lt.53
  3.1 0.1 copy.15
  3.2 0.8 copy.19
  4.0 0.1 reshape.123
  4.1 0.2 and_reduce_fusion
  4.3 0.7 broadcast_select_fusion
  5.0 0.2 copy.20
  5.2 0.1 reshape.124
  5.3 0.1 copy.18
  5.4 0.0 copy-start
  5.4 2.6 %copy-done = f32[12,7,128,128]{3,2,1,0:T(8,128)S(1)} copy-done((f32[12,7,128,128]{3,2,1,0:T(8,128)S(1)}, f32[12,7,128,128]{3,2,1,0:T(8,128)}, u32[]{:S(2)}) %copy-start) | copy-done | bytes 5505048
  7.9 0.0 copy-start.1
  7.9 0.9 copy-done.1
  8.8 85.3 %shard_map.73 = f32[3,8,8,128]{3,2,1,0:T(8,128)S(1)} custom-call(f32[84,128,128]{2,1,0:T(8,128)S(1)} %bitcast.23, f32[12,2,8,128]{3,2,1,0:T(8,128)S(1)} %copy-done.1, s32[8,128]{1,0:T(8,128)S(1)} %pad.8.tab, s32[24,128]{1,0:T(8,128)S(1)} %pad.9.slots, s32[84]{0:T(128)S(1)} %compare_select_fusion.pool_at, s32[12]{0:T(128)S(1)} %and_select_fusion.own_tag), custom_call_target="tpu_custom_call" | custom-call | tf_op jit(solution)/shard_map/pallas_call | solution.py:369
  94.1 0.6 copy.23
  (6 shorter events, 0.1 us)
Async XLA Ops:
  5.4 2.6 %copy-start = (f32[12,7,128,128]{3,2,1,0:T(8,128)S(1)}, f32[12,7,128,128]{3,2,1,0:T(8,128)}, u32[]{:S(2)}) copy-start(f32[12,7,128,128]{3,2,1,0:T(8,128)} %param.7) | copy-start | bytes 16515076
  7.9 0.9 copy-start.1

commit v2 on v1

v2 whole, which is shorter than its diff:
```python
import functools

import jax
import jax.numpy as jnp
from jax import lax
from jax.experimental import pallas as pl
from jax.experimental.pallas import tpu as pltpu
from jax.sharding import PartitionSpec as P

NX, NC = 4, 2
KC = 8
CR = 3
A8 = 8
LANES = 128
HALVES = 2
STAGES = 4
F32, BF16, I32 = jnp.float32, jnp.bfloat16, jnp.int32
NT = (((1,), (1,)), ((), ()))
NN = (((1,), (0,)), ((), ()))
MESH = pl.DeviceIdType.MESH


def split(v):
    high = v.astype(BF16)
    return high, (v - high.astype(F32)).astype(BF16)


def wide(v):
    high, low = split(v)
    return jnp.concatenate(
        [jnp.concatenate([high, high], axis=1), jnp.concatenate([low, jnp.zeros_like(low)], axis=1)], axis=0
    )


def steps_of(count, half):
    plus = count // 2 if half % 2 == 0 else count // 2 - 1
    return plus, count - 1 - plus


def ring_ids(count, halves):
    ids = {}
    for half in range(halves):
        for way, steps in zip((1, -1), steps_of(count, half)):
            for step in range(steps):
                ids[half, way, step] = len(ids)
    return ids


def kernel(
    dims, fine, prolong, cols, lengths, agg, coarse, plan, out,
    blocks, cut, whole, column, plans, plans_s, tabs, tabs_s, cols_s, lengths_s, agg_s, coarse_s,
    picked, pool, applied, wided, far_a, far_b, far_c, far_d, own, acc, crossed, running,
    local_sem, tab_send, tab_recv, z_send, z_recv, y_send, y_recv, g_send, g_recv,
    x_send, x_recv, c_send, c_recv, r_send, r_recv,
):
    NY, NZ, FR, KA = dims
    group = NX * NC
    per = NY + 1
    NB = NZ * A8
    EC = KC // STAGES
    hr = FR // HALVES
    y_steps, z_steps = NY // 2, NZ // 2
    far = (far_a, far_b, far_c, far_d)
    row, z = lax.axis_index("rows"), lax.axis_index("cols")
    core, x, y = row % NC, (row // NC) % NX, row // group
    here = x * NC + core

    def rid(yy, xx, cc):
        return (yy * NX + xx) * NC + cc

    def copy(src, dst, send, recv, device):
        return pltpu.make_async_remote_copy(
            src_ref=src, dst_ref=dst, send_sem=send, recv_sem=recv, device_id=device, device_id_type=MESH
        )

    def z_dev(way):
        return (row, (z + way + NZ) % NZ)

    def y_dev(way):
        return (rid((y + way + NY) % NY, x, core), z)

    def x_dev(way):
        return (rid(y, (x + way + NX) % NX, core), z)

    def g_dev(o):
        return (rid(y, (x + o // NC) % NX, (core + o % NC) % NC), z)

    core_dev = (rid(y, x, (core + 1) % NC), z)

    def bring(n, src, dst):
        c = pltpu.make_async_copy(src, dst, local_sem.at[n])
        c.start()
        return c

    got_prolong = bring(0, prolong, whole.at[z])
    got_plan = bring(1, plan, plans.at[y])
    got_agg = bring(2, agg, agg_s)
    got_cols = bring(3, cols, cols_s)
    got_lengths = bring(4, lengths, lengths_s)
    got_coarse = bring(5, coarse, coarse_s)
    got_fine = bring(6, fine, blocks)

    barrier = pltpu.get_barrier_semaphore()
    partners = [z_dev(o) for o in sorted({1, NZ - 1})]
    partners += [y_dev(o) for o in range(1, NY)]
    partners += [g_dev(o) for o in range(1, group)]
    for device in partners:
        pl.semaphore_signal(barrier, inc=1, device_id=device, device_id_type=MESH)
    got_prolong.wait()
    got_plan.wait()
    pl.semaphore_wait(barrier, len(partners))

    sent = []

    def go(c):
        c.start()
        sent.append(c)

    z_ids, y_ids = ring_ids(NZ, HALVES), ring_ids(NY, HALVES)

    def rows_of(half):
        return pl.ds(half * hr, hr)

    def ring_send(buf, ids, send, recv, me, count, dev, half, way, step):
        at = (me - way * step + count) % count
        part = whole.at[z, rows_of(half)] if step == 0 else buf.at[at, rows_of(half)]
        n = ids[half, way, step]
        go(copy(part, buf.at[at, rows_of(half)], send.at[n], recv.at[n], dev(way)))

    def ring_wait(buf, ids, send, recv, me, count, dev, half, way, step):
        at = (me - way * (step + 1) + 2 * count) % count
        part = buf.at[at, rows_of(half)]
        n = ids[half, way, step]
        copy(part, part, send.at[n], recv.at[n], dev(way)).wait_recv()

    zr = (whole, z_ids, z_send, z_recv, z, NZ, z_dev)
    yr = (column, y_ids, y_send, y_recv, y, NY, y_dev)

    def advance(ring, ids, step):
        for half in range(HALVES):
            for way in (1, -1):
                if (half, way, step) in ids:
                    ring_wait(*ring, half, way, step)
                    if (half, way, step + 1) in ids:
                        ring_send(*ring, half, way, step + 1)

    for half in range(HALVES):
        for way in (1, -1):
            if (half, way, 0) in y_ids:
                ring_send(*yr, half, way, 0)
            if (half, way, 0) in z_ids:
                ring_send(*zr, half, way, 0)
    for o in range(1, NY):
        go(copy(plans.at[y], plans.at[y], tab_send.at[o], tab_recv.at[o], y_dev(o)))
    column[y] = whole[z]
    pool[pl.ds(0, FR)] = whole[z]

    lane = lax.broadcasted_iota(I32, (8, LANES), 1)
    sub = lax.broadcasted_iota(I32, (8, LANES), 0)
    got_agg.wait()
    held = jnp.zeros((8, LANES), I32)
    tag = jnp.zeros((8, LANES), I32)
    for i in range(FR):
        off = agg_s[1, i] - CR * lane
        hit = (off >= 0) & (off < CR)
        held = jnp.where(hit, i, held)
        tag = jnp.where(hit, off + 1, tag)
    tabs[x] = jnp.where(sub == 0, held, tag)
    for o in range(1, NX):
        go(copy(tabs.at[x], tabs.at[x], tab_send.at[NY + o], tab_recv.at[NY + o], x_dev(o)))

    def name_pairs():
        got_cols.wait()
        got_lengths.wait()

        def name(i, both):
            for k in range(KA):
                off = jnp.where(k < lengths_s[0, i], cols_s[k, i], 0) - FR - 2 * lane
                both = tuple(jnp.where(off == c, 1, both[c]) for c in range(2))
            return both

        none = jnp.zeros((8, LANES), I32)
        named = lax.fori_loop(0, FR, name, (none, none))
        tabs[NX] = named[0] * named[1]

    def cut_blocks(leg):
        @pl.loop(FR * leg // 3, FR * (leg + 1) // 3)
        def _(i):
            for k in range(KA):
                high, low = split(blocks[i * KA + k])
                cut[i * KA + k] = jnp.concatenate([high, low], axis=1)

    def pick(o, put):
        dest = rid(y, (x + o // NC) % NX, (core + o % NC) % NC)
        extra_y, extra_row = 0, 0
        for yy in range(NY):
            first, second = plans_s[yy, 0, dest], plans_s[yy, 1, dest]
            put(yy, column[yy, jnp.where(first >= 0, first, jnp.maximum(second, 0))])
            both = jnp.minimum(first, second) >= 0
            extra_y = jnp.where(both, yy, extra_y)
            extra_row = jnp.where(both, second, extra_row)
        put(NY, column[extra_y, extra_row])

    def g_copy(o, src, h):
        return copy(src, pool.at[pl.ds(FR + h * per, per)], g_send.at[o], g_recv.at[o], g_dev(o))

    for step in range(y_steps):
        advance(yr, y_ids, step)
        if step < z_steps - 1:
            advance(zr, z_ids, step)
        if step == 0:
            name_pairs()
        if step == y_steps - 2:
            got_fine.wait()
            cut_blocks(0)
    if y_steps < 2:
        got_fine.wait()
        cut_blocks(0)
    for o in range(1, NY):
        at = plans.at[(y - o + NY) % NY]
        copy(at, at, tab_send.at[o], tab_recv.at[o], y_dev(o)).wait_recv()
    plans_in = bring(1, plans, plans_s)
    plans_in.wait()
    for o in list(range(1, group)) + [0]:
        if o:
            def put(n, v, o=o):
                picked[o, n] = v
        else:
            def put(n, v):
                pool[FR + here * per + n] = v
        pick(o, put)
        if o:
            go(g_copy(o, picked.at[o], here))
    z_next = min(y_steps, z_steps - 1)
    for leg in (1, 2):
        if z_next < z_steps - 1:
            advance(zr, z_ids, z_next)
            z_next += 1
        cut_blocks(leg)
    for o in range(1, NX):
        at = tabs.at[(x - o + NX) % NX]
        copy(at, at, tab_send.at[NY + o], tab_recv.at[NY + o], x_dev(o)).wait_recv()
    tabs_in = bring(2, tabs, tabs_s)

    got_coarse.wait()
    while z_next < z_steps - 1:
        advance(zr, z_ids, z_next)
        z_next += 1
    tabs_in.wait()
    for o in range(1, group):
        src = ((x - o // NC + NX) % NX) * NC + (core - o % NC + NC) % NC
        g_copy(o, pool.at[pl.ds(FR + src * per, per)], src).wait_recv()

    r8 = lax.broadcasted_iota(I32, (KC * A8, LANES), 0)
    l8 = lax.broadcasted_iota(I32, (KC * A8, LANES), 1)
    same_a = (r8 % A8) == (l8 % A8)
    slot_row = lax.broadcasted_iota(I32, (KC, A8, LANES), 0)
    lane_ks = lane // A8

    def couple(i):
        for k in range(KA):
            c = cols_s[k, i]
            ghost = jnp.maximum(c - FR, 0)
            q, odd = lax.div(ghost, 2), lax.rem(ghost, 2)
            slot = lax.div(q, group)
            slot = jnp.where(odd * tabs_s[NX, 0, q] > 0, NY, slot)
            at = jnp.where(c < FR, c, FR + lax.rem(q, group) * per + slot)
            lhs = wide(pool[at].reshape(2 * A8, LANES))
            both = lax.dot_general(lhs, cut[i * KA + k], NT, preferred_element_type=F32)
            applied[i, 2 * A8 * k:2 * A8 * (k + 1)] = both[:2 * A8] + both[2 * A8:]
        applied[i, 2 * A8 * KA:] = jnp.zeros((LANES - 2 * A8 * KA, LANES), F32)
        xh, xl = split(applied[i])
        rhs = jnp.concatenate([xh, xl], axis=0)
        for t in range(2):
            v = jnp.full((8, LANES), -1, I32)
            for k in range(KA):
                for s in range(2):
                    slot = jnp.where(k < lengths_s[0, i], coarse_s[t, k, s, i], -1)
                    v = jnp.where(lane_ks == 2 * k + s, slot, v)
            hit = (v[None] == slot_row).reshape(KC * A8, LANES) & same_a
            where = jnp.where(hit, 1.0, 0.0).astype(BF16)
            summed = lax.dot_general(
                jnp.concatenate([where, where], axis=1), rhs, NN, preferred_element_type=F32
            )
            wided[i, t] = wide(summed)

    def product(i, t):
        high, low = split(whole[:, i, t].reshape(NB, LANES))
        both = lax.dot_general(
            wided[i, t], jnp.concatenate([high, low], axis=1), NT, preferred_element_type=F32
        )
        return (both[:KC * A8] + both[KC * A8:]).reshape(KC, A8, NB)

    @pl.loop(0, FR)
    def _(i):
        couple(i)

    advance(zr, z_ids, z_steps - 1)

    @pl.loop(0, FR)
    def _(i):
        made = product(i, 1)
        for stage in range(STAGES):
            far[stage][x, i] = made[stage * EC:(stage + 1) * EC]

    def x_copy(stage, o, at):
        n = stage * NX + o
        return copy(far[stage].at[at], far[stage].at[at], x_send.at[n], x_recv.at[n], x_dev(o))

    def x_start(stage):
        for o in range(1, NX):
            if stage:
                x_copy(stage - 1, o, x).wait_send()
            x_copy(stage, o, x).start()

    def x_wait(stage):
        for o in range(1, NX):
            x_copy(stage, o, (x - o + NX) % NX).wait_recv()

    def c_copy(stage):
        return copy(
            acc.at[(core + 1) % NC, stage], crossed.at[stage], c_send.at[stage], c_recv.at[stage], core_dev
        )

    def combine(stage):
        for cc in range(NC):
            @pl.loop(0, NY)
            def _(yy):
                dest = rid(yy, x, cc)
                sums = [jnp.zeros((EC, A8, NB), F32) for _ in range(CR)]
                for xx in range(NX):
                    rows = far[stage][xx, tabs_s[xx, 0, dest]]
                    tag = tabs_s[xx, 1, dest]
                    for c in range(CR):
                        sums[c] += rows * jnp.where(tag == c + 1, 1.0, 0.0)
                for c in range(CR):
                    acc[cc, stage, yy, c] = sums[c]

        go(c_copy(stage))

    def r_copy(stage, o):
        n = stage * NY + o
        return copy(
            crossed.at[stage, (y + o) % NY], running.at[stage, o], r_send.at[n], r_recv.at[n], y_dev(o)
        )

    def r_start(stage):
        c_copy(stage).wait_recv()
        for o in sorted(range(1, NY), key=lambda o: -min(o, NY - o)):
            crossed[stage, (y + o) % NY] += acc[core, stage, (y + o) % NY]
            go(r_copy(stage, o))

    def finish(stage):
        total = own[:, stage * EC:(stage + 1) * EC] + crossed[stage, y] + acc[core, stage, y]
        for o in range(1, NY):
            r_copy(stage, o).wait_recv()
            total += running[stage, o]
        out[:, stage * EC:(stage + 1) * EC] = total

    x_start(0)
    own[...] = jnp.zeros_like(own)

    @pl.loop(0, FR)
    def _(i):
        made = product(i, 0)
        for c in range(CR):
            own[c] += made * jnp.where(agg_s[0, i] == row * CR + c, 1.0, 0.0)

    x_start(1)
    for stage in range(STAGES):
        x_wait(stage)
        if stage + 2 < STAGES:
            x_start(stage + 2)
        combine(stage)
        r_start(stage)
    for stage in range(STAGES):
        finish(stage)
    for o in range(1, NX):
        x_copy(STAGES - 1, o, x).wait_send()

    for c in sent:
        c.wait_send()


def per_device(fine_blocks, block_cols, row_length, prolong, aggregates, coarse_slot, send_plan):
    peers, NZ = lax.axis_size("rows"), lax.axis_size("cols")
    FR, KA = fine_blocks.shape[:2]
    group = NX * NC
    NY = peers // group
    per = NY + 1
    NB = NZ * A8
    EC = KC // STAGES

    hbm = pl.BlockSpec(memory_space=pltpu.HBM)
    count_z, count_y = len(ring_ids(NZ, HALVES)), len(ring_ids(NY, HALVES))
    dma = pltpu.SemaphoreType.DMA
    return pl.pallas_call(
        functools.partial(kernel, (NY, NZ, FR, KA)),
        out_shape=jax.ShapeDtypeStruct((CR, KC, A8, NB), F32),
        in_specs=[hbm] * 7,
        out_specs=pl.BlockSpec(memory_space=pltpu.VMEM),
        scratch_shapes=[
            pltpu.VMEM((FR * KA, LANES, LANES), F32),
            pltpu.VMEM((FR * KA, LANES, 2 * LANES), BF16),
            pltpu.VMEM((NZ, FR, 2, A8, LANES), F32),
            pltpu.VMEM((NY, FR, 2, A8, LANES), F32),
            pltpu.VMEM((NY, 2, peers), I32),
            pltpu.SMEM((NY, 2, peers), I32),
            pltpu.VMEM((NX + 1, 8, LANES), I32),
            pltpu.SMEM((NX + 1, 8, LANES), I32),
            pltpu.SMEM((KA, FR), I32),
            pltpu.SMEM((1, FR), I32),
            pltpu.SMEM((2, FR), I32),
            pltpu.SMEM((2, KA, 2, FR), I32),
            pltpu.VMEM((group, per, 2, A8, LANES), F32),
            pltpu.VMEM((FR + group * per, 2, A8, LANES), F32),
            pltpu.VMEM((FR, LANES, LANES), F32),
            pltpu.VMEM((FR, 2, 2 * KC * A8, 2 * LANES), BF16),
            *[pltpu.VMEM((NX, FR, EC, A8, NB), F32) for _ in range(STAGES)],
            pltpu.VMEM((CR, KC, A8, NB), F32),
            pltpu.VMEM((NC, STAGES, NY, CR, EC, A8, NB), F32),
            pltpu.VMEM((STAGES, NY, CR, EC, A8, NB), F32),
            pltpu.VMEM((STAGES, NY, CR, EC, A8, NB), F32),
            dma((7,)), dma((NY + NX,)), dma((NY + NX,)), dma((count_z,)), dma((count_z,)),
            dma((count_y,)), dma((count_y,)), dma((group,)), dma((group,)),
            dma((STAGES * NX,)), dma((STAGES * NX,)), dma((STAGES,)), dma((STAGES,)),
            dma((STAGES * NY,)), dma((STAGES * NY,)),
        ],
        compiler_params=pltpu.CompilerParams(
            collective_id=0, has_side_effects=True, vmem_limit_bytes=56 * 2**20
        ),
    )(
        fine_blocks.reshape(FR * KA, LANES, LANES), prolong, block_cols.T, row_length[None, :], aggregates.T,
        jnp.transpose(coarse_slot, (1, 2, 3, 0)), jnp.transpose(send_plan[0]),
    )


def solution(mesh):
    return jax.shard_map(
        per_device,
        mesh=mesh,
        in_specs=(
            P("rows", None, None, None),
            P("rows", None),
            P("rows"),
            P("rows", None, "cols", None),
            P("rows", None),
            P("rows", None, None, None),
            P("rows", None, None),
        ),
        out_specs=P("rows", None, "cols", None),
        check_vma=False,
    )
```

time: 95.7 us -> 90.6 us (0.947)
  local copies, waits for them, and re-layouts: 5.52 us -> 1.54 us
  other arithmetic: 3.91 us -> 0 us
  Pallas kernels: 85.3 us -> 88.9 us
    pallas_call x1, Pallas kernels: 85.3 us -> 88.9 us  [per_device(): pl.pallas_call(functools.partial(kernel, (NY, NZ, FR, KA)), out_shape=jax...]
    unnamed x6 -> x1, local copies, waits for them, and re-layouts: 4.89 us -> 1.54 us
    select_n x4 -> x0, other arithmetic: 2.2 us -> none  [the longest x1 0.76 us: per_device(): main = jnp.where(first >= 0, first, jnp.maximum(second, 0))]
where the time goes in v2:
time: 90.6 us; the launch traced here: 90.4 us
  Pallas kernels  88.9 us (98%)
  local copies, waits for them, and re-layouts  1.54 us (2%)
    pallas_call x1, Pallas kernels, per_device(): pl.pallas_call(functools.partial(kernel, (NY, NZ, FR, KA)), out_shape=jax...  88.9 us

profile of v2, /device:TPU:1, one launch (start us, length us, event | category | flops | bytes accessed | tf_op | source)
XLA Modules:
  0.0 90.4 jit_solution(329453923611860372)
XLA Ops:
  0.0 88.9 %shard_map.73 = f32[3,8,8,128]{3,2,1,0:T(8,128)} custom-call(f32[84,128,128]{2,1,0:T(8,128)} %bitcast.8, f32[12,2,8,128]{3,2,1,0:T(8,128)} %prolong.1, s32[7,12]{1,0:T(8,128)} %bitcast.10, s32[1,12]{1,0:T(1,128)} %bitcast.13, s32[2,12]{1,0:T(2,128)} %bitcast.11, s32[2,7,2,12]{3,2,1,0:T(2,128)} %bitcast.9, s32[2,64]{1,0:T(2,128)} %bitcast.12), custom_call_target="tpu_custom_call" | custom-call | tf_op jit(solution)/shard_map/pallas_call | solution.py:397
  88.9 1.5 %copy.9 = f32[3,8,8,128]{3,2,1,0:T(8,128)} copy(f32[3,8,8,128]{3,2,1,0:T(8,128)} %shard_map.73) | data formatting | bytes 196608

commit v3 on v2

--- a/solution.py
+++ b/solution.py
@@ -14,6 +14,7 @@
 LANES = 128
 HALVES = 2
 STAGES = 4
+UNROLL = 3
 F32, BF16, I32 = jnp.float32, jnp.bfloat16, jnp.int32
 NT = (((1,), (1,)), ((), ()))
 NN = (((1,), (0,)), ((), ()))
@@ -92,7 +93,8 @@
         c.start()
         return c
 
-    got_prolong = bring(0, prolong, whole.at[z])
+    got_rows = bring(0, prolong, column.at[y])
+    got_sides = [bring(7 + t, prolong.at[:, t], whole.at[t, z]) for t in range(2)]
     got_plan = bring(1, plan, plans.at[y])
     got_agg = bring(2, agg, agg_s)
     got_cols = bring(3, cols, cols_s)
@@ -101,12 +103,14 @@
     got_fine = bring(6, fine, blocks)
 
     barrier = pltpu.get_barrier_semaphore()
-    partners = [z_dev(o) for o in sorted({1, NZ - 1})]
+    partners = [z_dev(o) for o in sorted({1, 2, NZ - 2, NZ - 1} - {0, NZ})]
     partners += [y_dev(o) for o in range(1, NY)]
     partners += [g_dev(o) for o in range(1, group)]
     for device in partners:
         pl.semaphore_signal(barrier, inc=1, device_id=device, device_id_type=MESH)
-    got_prolong.wait()
+    got_rows.wait()
+    for c in got_sides:
+        c.wait()
     got_plan.wait()
     pl.semaphore_wait(barrier, len(partners))
 
@@ -116,16 +120,16 @@
         c.start()
         sent.append(c)
 
-    z_ids, y_ids = ring_ids(NZ, HALVES), ring_ids(NY, HALVES)
+    y_ids = ring_ids(NY, HALVES)
 
     def rows_of(half):
         return pl.ds(half * hr, hr)
 
     def ring_send(buf, ids, send, recv, me, count, dev, half, way, step):
         at = (me - way * step + count) % count
-        part = whole.at[z, rows_of(half)] if step == 0 else buf.at[at, rows_of(half)]
+        part = buf.at[at, rows_of(half)]
         n = ids[half, way, step]
-        go(copy(part, buf.at[at, rows_of(half)], send.at[n], recv.at[n], dev(way)))
+        go(copy(part, part, send.at[n], recv.at[n], dev(way)))
 
     def ring_wait(buf, ids, send, recv, me, count, dev, half, way, step):
         at = (me - way * (step + 1) + 2 * count) % count
@@ -133,7 +137,6 @@
         n = ids[half, way, step]
         copy(part, part, send.at[n], recv.at[n], dev(way)).wait_recv()
 
-    zr = (whole, z_ids, z_send, z_recv, z, NZ, z_dev)
     yr = (column, y_ids, y_send, y_recv, y, NY, y_dev)
 
     def advance(ring, ids, step):
@@ -148,12 +151,51 @@
         for way in (1, -1):
             if (half, way, 0) in y_ids:
                 ring_send(*yr, half, way, 0)
-            if (half, way, 0) in z_ids:
-                ring_send(*zr, half, way, 0)
+    z_reach = {(t, way): steps_of(NZ, t)[0 if way == 1 else 1] for t in range(2) for way in (1, -1)}
+    z_ids = {}
+    for t, way in z_reach:
+        for far_by in range(1, z_reach[t, way] + 1):
+            z_ids[t, way, far_by] = len(z_ids)
+
+    def z_copy(t, way, far_by, at):
+        n = z_ids[t, way, far_by]
+        part = whole.at[t, at]
+        return copy(part, part, z_send.at[n], z_recv.at[n], z_dev(way * (1 if far_by % 2 else 2)))
+
+    def z_push(t, base):
+        for hop in (2, 1):
+            for way in (1, -1):
+                if base + hop <= z_reach[t, way]:
+                    go(z_copy(t, way, base + hop, (z - way * base + NZ) % NZ))
+
+    def z_wait(t, far_by):
+        for way in (1, -1):
+            if far_by <= z_reach[t, way]:
+                z_copy(t, way, far_by, (z - way * far_by + NZ) % NZ).wait_recv()
+
+    def z_step(t, base):
+        z_wait(t, base)
+        z_push(t, base)
+
+    def z_rest(t):
+        for far_by in range(1, z_steps + 1):
+            if far_by % 2 or far_by == z_steps:
+                z_wait(t, far_by)
+
+    relays = list(range(2, z_steps, 2))
+    queue = []
+    for n, base in enumerate(relays):
+        queue += [(1, base)] + [(0, b) for b in relays[n - 1:n] if n]
+    queue += [(0, b) for b in relays[-1:]]
+
+    def z_next():
+        if queue:
+            z_step(*queue.pop(0))
+
+    z_push(1, 0)
     for o in range(1, NY):
         go(copy(plans.at[y], plans.at[y], tab_send.at[o], tab_recv.at[o], y_dev(o)))
-    column[y] = whole[z]
-    pool[pl.ds(0, FR)] = whole[z]
+    pool[pl.ds(0, FR)] = column[y]
 
     lane = lax.broadcasted_iota(I32, (8, LANES), 1)
     sub = lax.broadcasted_iota(I32, (8, LANES), 0)
@@ -206,9 +248,9 @@
 
     for step in range(y_steps):
         advance(yr, y_ids, step)
-        if step < z_steps - 1:
-            advance(zr, z_ids, step)
+        z_next()
         if step == 0:
+            z_push(0, 0)
             name_pairs()
         if step == y_steps - 2:
             got_fine.wait()
@@ -231,21 +273,17 @@
         pick(o, put)
         if o:
             go(g_copy(o, picked.at[o], here))
-    z_next = min(y_steps, z_steps - 1)
-    for leg in (1, 2):
-        if z_next < z_steps - 1:
-            advance(zr, z_ids, z_next)
-            z_next += 1
-        cut_blocks(leg)
+    cut_blocks(1)
+    z_next()
+    cut_blocks(2)
     for o in range(1, NX):
         at = tabs.at[(x - o + NX) % NX]
         copy(at, at, tab_send.at[NY + o], tab_recv.at[NY + o], x_dev(o)).wait_recv()
     tabs_in = bring(2, tabs, tabs_s)
 
     got_coarse.wait()
-    while z_next < z_steps - 1:
-        advance(zr, z_ids, z_next)
-        z_next += 1
+    while queue:
+        z_next()
     tabs_in.wait()
     for o in range(1, group):
         src = ((x - o // NC + NX) % NX) * NC + (core - o % NC + NC) % NC
@@ -285,19 +323,19 @@
             wided[i, t] = wide(summed)
 
     def product(i, t):
-        high, low = split(whole[:, i, t].reshape(NB, LANES))
+        high, low = split(whole[t, :, i].reshape(NB, LANES))
         both = lax.dot_general(
             wided[i, t], jnp.concatenate([high, low], axis=1), NT, preferred_element_type=F32
         )
         return (both[:KC * A8] + both[KC * A8:]).reshape(KC, A8, NB)
 
-    @pl.loop(0, FR)
+    @pl.loop(0, FR, unroll=UNROLL)
     def _(i):
         couple(i)
 
-    advance(zr, z_ids, z_steps - 1)
-
-    @pl.loop(0, FR)
+    z_rest(1)
+
+    @pl.loop(0, FR, unroll=UNROLL)
     def _(i):
         made = product(i, 1)
         for stage in range(STAGES):
@@ -309,8 +347,6 @@
 
     def x_start(stage):
         for o in range(1, NX):
-            if stage:
-                x_copy(stage - 1, o, x).wait_send()
             x_copy(stage, o, x).start()
 
     def x_wait(stage):
@@ -357,15 +393,18 @@
             total += running[stage, o]
         out[:, stage * EC:(stage + 1) * EC] = total
 
+    def own_products():
+        own[...] = jnp.zeros_like(own)
+        z_rest(0)
+
+        @pl.loop(0, FR)
+        def _(i):
+            made = product(i, 0)
+            for c in range(CR):
+                own[c] += made * jnp.where(agg_s[0, i] == row * CR + c, 1.0, 0.0)
+
     x_start(0)
-    own[...] = jnp.zeros_like(own)
-
-    @pl.loop(0, FR)
-    def _(i):
-        made = product(i, 0)
-        for c in range(CR):
-            own[c] += made * jnp.where(agg_s[0, i] == row * CR + c, 1.0, 0.0)
-
+    own_products()
     x_start(1)
     for stage in range(STAGES):
         x_wait(stage)
@@ -375,8 +414,9 @@
         r_start(stage)
     for stage in range(STAGES):
         finish(stage)
-    for o in range(1, NX):
-        x_copy(STAGES - 1, o, x).wait_send()
+    for stage in range(STAGES):
+        for o in range(1, NX):
+            x_copy(stage, o, x).wait_send()
 
     for c in sent:
         c.wait_send()
@@ -392,7 +432,7 @@
     EC = KC // STAGES
 
     hbm = pl.BlockSpec(memory_space=pltpu.HBM)
-    count_z, count_y = len(ring_ids(NZ, HALVES)), len(ring_ids(NY, HALVES))
+    count_z, count_y = 2 * (NZ - 1), len(ring_ids(NY, HALVES))
     dma = pltpu.SemaphoreType.DMA
     return pl.pallas_call(
         functools.partial(kernel, (NY, NZ, FR, KA)),
@@ -402,7 +442,7 @@
         scratch_shapes=[
             pltpu.VMEM((FR * KA, LANES, LANES), F32),
             pltpu.VMEM((FR * KA, LANES, 2 * LANES), BF16),
-            pltpu.VMEM((NZ, FR, 2, A8, LANES), F32),
+            pltpu.VMEM((2, NZ, FR, A8, LANES), F32),
             pltpu.VMEM((NY, FR, 2, A8, LANES), F32),
             pltpu.VMEM((NY, 2, peers), I32),
             pltpu.SMEM((NY, 2, peers), I32),
@@ -421,7 +461,7 @@
             pltpu.VMEM((NC, STAGES, NY, CR, EC, A8, NB), F32),
             pltpu.VMEM((STAGES, NY, CR, EC, A8, NB), F32),
             pltpu.VMEM((STAGES, NY, CR, EC, A8, NB), F32),
-            dma((7,)), dma((NY + NX,)), dma((NY + NX,)), dma((count_z,)), dma((count_z,)),
+            dma((9,)), dma((NY + NX,)), dma((NY + NX,)), dma((count_z,)), dma((count_z,)),
             dma((count_y,)), dma((count_y,)), dma((group,)), dma((group,)),
             dma((STAGES * NX,)), dma((STAGES * NX,)), dma((STAGES,)), dma((STAGES,)),
             dma((STAGES * NY,)), dma((STAGES * NY,)),

time: 90.6 us -> 84.3 us (0.930)
  Pallas kernels: 88.9 us -> 82.6 us
    pallas_call x1, Pallas kernels: 88.9 us -> 82.6 us  [per_device(): pl.pallas_call(functools.partial(kernel, (NY, NZ, FR, KA)), out_shape=jax...]
where the time goes in v3:
time: 84.3 us; the launch traced here: 84.1 us
  Pallas kernels  82.6 us (98%)
  local copies, waits for them, and re-layouts  1.54 us (2%)
    pallas_call x1, Pallas kernels, per_device(): pl.pallas_call(functools.partial(kernel, (NY, NZ, FR, KA)), out_shape=jax...  82.6 us

profile of v3, /device:TPU:1, one launch (start us, length us, event | category | flops | bytes accessed | tf_op | source)
XLA Modules:
  0.0 84.1 jit_solution(12096933361210326469)
XLA Ops:
  0.0 82.6 %shard_map.73 = f32[3,8,8,128]{3,2,1,0:T(8,128)} custom-call(f32[84,128,128]{2,1,0:T(8,128)} %bitcast.8, f32[12,2,8,128]{3,2,1,0:T(8,128)} %prolong.1, s32[7,12]{1,0:T(8,128)} %bitcast.10, s32[1,12]{1,0:T(1,128)} %bitcast.13, s32[2,12]{1,0:T(2,128)} %bitcast.11, s32[2,7,2,12]{3,2,1,0:T(2,128)} %bitcast.9, s32[2,64]{1,0:T(2,128)} %bitcast.12), custom_call_target="tpu_custom_call" | custom-call | tf_op jit(solution)/shard_map/pallas_call | solution.py:437
  82.6 1.5 %copy.9 = f32[3,8,8,128]{3,2,1,0:T(8,128)} copy(f32[3,8,8,128]{3,2,1,0:T(8,128)} %shard_map.73) | data formatting | bytes 196608
